TPU v7x, 128 devices: a whole 4x4x4 slice. The times are simulated.
128 devices in a mesh: section: 4 (over y), expert: 32 (over x, z, core).
Axes of the slice: x: 4, y: 4, z: 4, core: 2. Of those that a mesh axis runs over, the one named last changes fastest.
Arguments:
- saved_inputs: bfloat16 [4, 2, 2048, 4096], P('section', None, 'expert'), may hold values from -6 to 6
- arriving: bfloat16 [4, 2048, 4096], P('section', 'expert'), may hold values from -1.5 to 1.5
- last_grad: bfloat16 [2048, 4096], P('expert'), may hold values from -1.5 to 1.5
- expert_ids: int32 [4, 2, 2048, 3], P('section', None, 'expert'), may hold values from 0 to 15, all different within a row; in each aligned block of 64 rows (0 to 63, 64 to 127, ..., all dimensions but the last counted through in order) at most 14 rows name the same one
- combine: bfloat16 [4, 2, 2048, 3], P('section', None, 'expert'), may hold values from 0.099609375 to 1
- w_gate: bfloat16 [4, 32, 4096, 384], P('section', 'expert'), may hold values from -0.09375 to 0.09375
- w_up: bfloat16 [4, 32, 4096, 384], P('section', 'expert'), may hold values from -0.09375 to 0.09375
- w_down: bfloat16 [4, 32, 384, 4096], P('section', 'expert'), may hold values from -0.21875 to 0.21875
Outputs:
- first_grads: bfloat16 [4, 2048, 4096], P('section', 'expert')
- second_grads: bfloat16 [4, 2048, 4096], P('section', 'expert')
- grad_gate: bfloat16 [4, 32, 4096, 384], P('section', 'expert')
- grad_up: bfloat16 [4, 32, 4096, 384], P('section', 'expert')
- grad_down: bfloat16 [4, 32, 384, 4096], P('section', 'expert')
Inputs may be any that keep to these rules, and one draw needn't show every extreme that they name: `expert_ids`: each token names 3 different experts. In every aligned block of 64 tokens (the tokens of one device in one section and micro-batch) no expert is named by more than 14 tokens, and in some blocks one expert is named by exactly 14.
All inputs are finite; a program needn't handle non-finite values.
Results may differ from a plain program's by a relative error of at most 0.0085.
Values may be sent and summed in bfloat16 or wider, within the bound.
A program may use at most 192 MiB of HBM per device.

v0:
```python
import jax
import jax.numpy as jnp
from jax import lax
from jax.sharding import PartitionSpec as P

HALVES = 2


def shifted(value, axis, by):
    count = lax.axis_size(axis)
    pairs = [(i, i + by) for i in range(count) if 0 <= i + by < count]
    return lax.ppermute(value, axis, pairs)


def rows_backward(x_rows, weighted, gate_w, up_w, down_w):
    gate_pre = jnp.dot(x_rows, gate_w, preferred_element_type=jnp.float32)
    up_pre = jnp.dot(x_rows, up_w, preferred_element_type=jnp.float32)
    gate_sigmoid = jax.nn.sigmoid(gate_pre)
    active = gate_pre * gate_sigmoid
    hidden = (active * up_pre).astype(jnp.bfloat16)
    contract = (((1,), (1,)), ((), ()))
    hidden_grad = lax.dot_general(weighted, down_w, contract, preferred_element_type=jnp.float32)
    gate_rows = (
        hidden_grad * up_pre * gate_sigmoid * (1.0 + gate_pre * (1.0 - gate_sigmoid))
    ).astype(jnp.bfloat16)
    up_rows = (hidden_grad * active).astype(jnp.bfloat16)
    partial_value = lax.dot_general(gate_rows, gate_w, contract, preferred_element_type=jnp.float32)
    partial_value = partial_value + lax.dot_general(
        up_rows, up_w, contract, preferred_element_type=jnp.float32
    )
    return (partial_value, hidden, gate_rows, up_rows)


def weight_terms(pieces):
    x_rows, weighted, hidden, gate_rows, up_rows = pieces
    across = (((0,), (0,)), ((), ()))
    return (
        lax.dot_general(x_rows, gate_rows, across, preferred_element_type=jnp.float32),
        lax.dot_general(x_rows, up_rows, across, preferred_element_type=jnp.float32),
        lax.dot_general(hidden, weighted, across, preferred_element_type=jnp.float32),
    )


def route_targets(route_ids, experts, capacity):
    tokens, top_count = route_ids.shape
    flat_ids = route_ids.reshape(tokens * top_count)
    onehot = (flat_ids[:, None] == jnp.arange(experts, dtype=jnp.int32)[None, :]).astype(jnp.int32)
    before = jnp.cumsum(onehot, axis=0) - onehot
    slot_index = jnp.sum(before * onehot, axis=1)
    return (flat_ids * capacity + slot_index).reshape(tokens, top_count)


def local(saved_inputs, arriving, last_grad, expert_ids, combine, w_gate, w_up, w_down):
    gate_w = w_gate[0, 0]
    up_w = w_up[0, 0]
    down_w = w_down[0, 0]
    tok_dev = arriving.shape[1]
    model_width = arriving.shape[2]
    top_count = expert_ids.shape[3]
    shards = lax.axis_size("expert")
    experts = shards // HALVES
    capacity = 5 * tok_dev * top_count // (4 * experts) // 2 * 2

    def section_pass(inputs, grads_in, route_ids, weights):
        target = route_targets(route_ids, experts, capacity)
        positions = jnp.arange(experts * capacity, dtype=jnp.int32)
        placed = target[None, :, :] == positions[:, None, None]
        picked = jnp.any(placed, axis=2).astype(jnp.bfloat16)
        scaled = jnp.sum(
            jnp.where(placed, weights[None, :, :].astype(jnp.float32), 0.0), axis=2
        ).astype(jnp.bfloat16)
        tables = jnp.stack([picked, scaled])
        sources = jnp.stack([inputs, grads_in])
        payload = jnp.einsum(
            "pqt,ptd->pqd", tables, sources, preferred_element_type=jnp.float32
        ).astype(jnp.bfloat16)
        spread = jnp.broadcast_to(
            payload.reshape(2, experts, 1, capacity, model_width),
            (2, experts, HALVES, capacity, model_width),
        )
        arrived = lax.all_to_all(
            spread.reshape(2, shards, capacity, model_width),
            "expert",
            split_axis=1,
            concat_axis=1,
            tiled=True,
        )
        x_rows = arrived[0].reshape(shards * capacity, model_width)
        weighted = arrived[1].reshape(shards * capacity, model_width)
        partial_value, hidden, gate_rows, up_rows = rows_backward(
            x_rows, weighted, gate_w, up_w, down_w
        )
        partial_value = partial_value.reshape(shards, capacity, model_width)
        returned_rows = lax.all_to_all(
            partial_value, "expert", split_axis=0, concat_axis=0, tiled=True
        )
        expert_rows = jnp.sum(
            returned_rows.reshape(experts, HALVES, capacity, model_width), axis=1
        ).astype(jnp.bfloat16)
        collect = jnp.any(target[:, :, None] == positions[None, None, :], axis=1).astype(
            jnp.bfloat16
        )
        expert_sum = jnp.dot(
            collect,
            expert_rows.reshape(experts * capacity, model_width),
            preferred_element_type=jnp.float32,
        )
        result = (grads_in.astype(jnp.float32) + expert_sum).astype(jnp.bfloat16)
        return (result, (x_rows, weighted, hidden, gate_rows, up_rows))

    section_last = lax.axis_index("section") == lax.axis_size("section") - 1
    first_grad, kept_first = section_pass(
        saved_inputs[0, 0], arriving[0], expert_ids[0, 0], combine[0, 0]
    )
    totals = weight_terms(kept_first)
    passed = shifted(first_grad, "section", -1)
    incoming = jnp.where(section_last, last_grad, passed)
    second_grad, kept_second = section_pass(
        saved_inputs[0, 1], incoming, expert_ids[0, 1], combine[0, 1]
    )
    second_terms = weight_terms(kept_second)
    totals = tuple((pair[0] + pair[1] for pair in zip(totals, second_terms)))
    return (
        first_grad[None],
        second_grad[None],
        totals[0].astype(jnp.bfloat16)[None, None],
        totals[1].astype(jnp.bfloat16)[None, None],
        totals[2].astype(jnp.bfloat16)[None, None],
    )


def solution(mesh):
    return jax.shard_map(
        local,
        mesh=mesh,
        in_specs=(
            P("section", None, "expert", None),
            P("section", "expert", None),
            P("expert", None),
            P("section", None, "expert", None),
            P("section", None, "expert", None),
            P("section", "expert", None, None),
            P("section", "expert", None, None),
            P("section", "expert", None, None),
        ),
        out_specs=(
            P("section", "expert", None),
            P("section", "expert", None),
            P("section", "expert", None, None),
            P("section", "expert", None, None),
            P("section", "expert", None, None),
        ),
        check_vma=False,
    )
```

profile of v0, /device:TPU:52, one launch (start us, length us, event | category | flops | bytes accessed | tf_op | source)
XLA Modules:
  0.0 666.0 jit_solution(7968685927313758433)
XLA Ops:
  13.5 7.1 %broadcast_in_dim.56 = bf16[2,16,2,14,4096]{4,0,3,2,1:T(2,128)(2,1)S(1)} broadcast(bf16[2,16,14,4096]{3,0,2,1:T(2,128)(2,1)S(1)} %bitcast.125), dimensions={0,1,3,4} | broadcast | bytes 11010048 | tf_op jit(solution)/shard_map/broadcast_in_dim | solution.py:77
  20.6 89.6 %all_to_all.20 = bf16[2,32,14,4096]{3,0,2,1:T(2,128)(2,1)S(1)} all-to-all(bf16[2,32,14,4096]{3,0,2,1:T(2,128)(2,1)S(1)} %bitcast.123), channel_id=1, replica_groups=mesh['section'=4,'expert'=32] {'expert'}, dimensions={1} | all-to-all | bytes 14680064 | tf_op jit(solution)/shard_map/all_to_all | solution.py:81
  110.2 36.9 %slice_reduce_fusion.3 = (bf16[32,14,4096]{2,1,0:T(8,128)(2,1)}, bf16[32,14,4096]{2,1,0:T(8,128)(2,1)}) fusion(bf16[2,32,14,4096]{3,0,2,1:T(2,128)(2,1)S(1)} %all_to_all.20), kind=kLoop, calls=%fused_computation.5 | loop fusion | bytes 14680064 | tf_op jit(solution)/shard_map/slice | solution.py:89
  152.1 5.1 fusion.10
  160.1 5.1 reshape_squeeze.14
  165.2 5.5 multiply_convert_fusion.4
  172.9 5.2 convolution_add_fusion.1
  178.1 6.9 %reshape.163 = f32[32,14,4096]{2,1,0:T(8,128)} reshape(f32[448,4096]{1,0:T(8,128)} %convolution_add_fusion.1) | data formatting | bytes 14680064 | tf_op jit(solution)/shard_map/reshape | solution.py:93
  184.9 8.0 %all-to-all-start.1 = ((f32[32,14,4096]{2,1,0:T(8,128)}), f32[32,14,4096]{2,1,0:T(8,128)}, u32[]{:S(2)}, u32[]{:S(2)}) async-start(f32[32,14,4096]{2,1,0:T(8,128)} %reshape.163), calls=%async_computation.1 | async-start | bytes 16777216 | tf_op jit(solution)/shard_map/all_to_all | solution.py:94
  193.1 124.2 %all-to-all-done.1 = f32[32,14,4096]{2,1,0:T(8,128)} async-done(((f32[32,14,4096]{2,1,0:T(8,128)}), f32[32,14,4096]{2,1,0:T(8,128)}, u32[]{:S(2)}, u32[]{:S(2)}) %all-to-all-start.1) | async-done | bytes 7340064 | tf_op jit(solution)/shard_map/all_to_all | solution.py:94
  317.3 6.0 bitcast_reduce_fusion.1
  331.6 12.8 %collective-permute-done = bf16[64,4096]{1,0:T(8,128)(2,1)} collective-permute-done((bf16[64,4096]{1,0:T(8,128)(2,1)}, bf16[64,4096]{1,0:T(8,128)(2,1)}, u32[]{:S(2)}, u32[]{:S(2)}) %collective-permute-start) | collective-permute-done | bytes 524320 | tf_op jit(solution)/shard_map/ppermute | solution.py:12
  351.6 7.1 %broadcast_in_dim.60 = bf16[2,16,2,14,4096]{4,0,3,2,1:T(2,128)(2,1)S(1)} broadcast(bf16[2,16,14,4096]{3,0,2,1:T(2,128)(2,1)S(1)} %bitcast.126), dimensions={0,1,3,4} | broadcast | bytes 11010048 | tf_op jit(solution)/shard_map/broadcast_in_dim | solution.py:77
  358.8 87.1 %all_to_all.21 = bf16[2,32,14,4096]{3,0,2,1:T(2,128)(2,1)S(1)} all-to-all(bf16[2,32,14,4096]{3,0,2,1:T(2,128)(2,1)S(1)} %bitcast.124), channel_id=1, replica_groups=mesh['section'=4,'expert'=32] {'expert'}, dimensions={1} | all-to-all | bytes 14680064 | tf_op jit(solution)/shard_map/all_to_all | solution.py:81
  445.9 36.9 %slice_reduce_fusion.1 = (bf16[32,14,4096]{2,1,0:T(8,128)(2,1)}, bf16[32,14,4096]{2,1,0:T(8,128)(2,1)}) fusion(bf16[2,32,14,4096]{3,0,2,1:T(2,128)(2,1)S(1)} %all_to_all.21), kind=kLoop, calls=%fused_computation.3 | loop fusion | bytes 14680064 | tf_op jit(solution)/shard_map/slice | solution.py:89
  482.8 5.0 reshape_squeeze.17
  487.8 6.1 fusion.13
  496.8 5.4 reshape_squeeze.16
  502.2 5.5 multiply_convert_fusion.2
  509.9 5.1 convolution_add_fusion
  515.0 6.8 %reshape.168 = f32[32,14,4096]{2,1,0:T(8,128)} reshape(f32[448,4096]{1,0:T(8,128)} %convolution_add_fusion) | data formatting | bytes 14680064 | tf_op jit(solution)/shard_map/reshape | solution.py:93
  521.8 8.2 %all-to-all-start.3 = ((f32[32,14,4096]{2,1,0:T(8,128)}), f32[32,14,4096]{2,1,0:T(8,128)}, u32[]{:S(2)}, u32[]{:S(2)}) async-start(f32[32,14,4096]{2,1,0:T(8,128)} %reshape.168), calls=%async_computation.3 | async-start | bytes 16777216 | tf_op jit(solution)/shard_map/all_to_all | solution.py:94
  551.8 102.3 %all-to-all-done.3 = f32[32,14,4096]{2,1,0:T(8,128)} async-done(((f32[32,14,4096]{2,1,0:T(8,128)}), f32[32,14,4096]{2,1,0:T(8,128)}, u32[]{:S(2)}, u32[]{:S(2)}) %all-to-all-start.3) | async-done | bytes 7340064 | tf_op jit(solution)/shard_map/all_to_all | solution.py:94
  654.1 6.1 bitcast_reduce_fusion
  (98 shorter events, 70.8 us)
Async XLA Ops:
  0.6 151.4 %copy-start = (bf16[1,1,4096,384]{3,2,1,0:T(8,128)(2,1)S(1)}, bf16[1,1,4096,384]{3,2,1,0:T(8,128)(2,1)}, u32[]{:S(2)}) copy-start(bf16[1,1,4096,384]{3,2,1,0:T(8,128)(2,1)} %param.13) | copy-start | bytes 9437188
  152.1 5.1 copy-start.3
  152.1 5.1 copy-start.7
  170.7 2.1 copy-start.12
  170.8 2.1 copy-start.8
  184.9 132.3 %all-to-all-start.1 = ((f32[32,14,4096]{2,1,0:T(8,128)}), f32[32,14,4096]{2,1,0:T(8,128)}, u32[]{:S(2)}, u32[]{:S(2)}) async-start(f32[32,14,4096]{2,1,0:T(8,128)} %reshape.163), calls=%async_computation.1 | async-start | bytes 16777216 | tf_op jit(solution)/shard_map/all_to_all | solution.py:94
  328.8 15.7 %collective-permute-start = (bf16[64,4096]{1,0:T(8,128)(2,1)}, bf16[64,4096]{1,0:T(8,128)(2,1)}, u32[]{:S(2)}, u32[]{:S(2)}) collective-permute-start(bf16[64,4096]{1,0:T(8,128)(2,1)} %fusion.3), channel_id=1, source_target_pairs={{32,0},{64,32},{96,64},{33,1},{65,33},{97,65},{34,2},{66,34},{98,6... | collective-permute-start | bytes 1572872 | tf_op jit(solution)/shard_map/ppermute | solution.py:12
  487.8 6.1 copy-start.1
  507.7 2.1 copy-start.14
  507.7 2.1 copy-start.10
  507.7 2.1 copy-start.9
  521.8 132.3 %all-to-all-start.3 = ((f32[32,14,4096]{2,1,0:T(8,128)}), f32[32,14,4096]{2,1,0:T(8,128)}, u32[]{:S(2)}, u32[]{:S(2)}) async-start(f32[32,14,4096]{2,1,0:T(8,128)} %reshape.168), calls=%async_computation.3 | async-start | bytes 16777216 | tf_op jit(solution)/shard_map/all_to_all | solution.py:94
  530.1 4.7 copy-start.4
  530.1 4.7 copy-start.13
  534.8 2.5 copy-start.5
  534.8 2.5 copy-start.16
  534.8 2.5 copy-start.17
  537.3 2.0 copy-start.2
  537.3 2.1 copy-start.11
  539.4 4.2 copy-start.15
  543.6 4.2 copy-start.6
  543.6 4.2 copy-start.18
  543.6 4.2 copy-start.19
where the time goes:
time: 672 us; the launch traced here: 666 us
  waiting for transfers between devices  239 us (36%)
  blocking collectives  177 us (26%)
  local copies, waits for them, and re-layouts  139 us (21%)
  matrix products  74 us (11%)
  starting transfers between devices  18.7 us (3%)
  other arithmetic  16.9 us (3%)
    all_to_all x2, waiting for transfers between devices, section_pass(): lax.all_to_all(partial_value, 'expert', split_axis=0, concat_axis=0, tile...  227 us
    all_to_all x2, blocking collectives, section_pass(): lax.all_to_all(spread.reshape(2, shards, capacity, model_width), 'expert'...  177 us
    slice x2, local copies, waits for them, and re-layouts, section_pass(): weighted = arrived[1].reshape(shards * capacity, model_width)  73.9 us
    all_to_all x2, starting transfers between devices, section_pass(): lax.all_to_all(partial_value, 'expert', split_axis=0, concat_axis=0, tile...  16.2 us
    broadcast_in_dim x2, local copies, waits for them, and re-layouts, section_pass(): jnp.broadcast_to(payload.reshape(2, experts, 1, capacity, model_width), (...  14.2 us
    reshape x2, local copies, waits for them, and re-layouts, section_pass(): partial_value = partial_value.reshape(shards, capacity, model_width)  13.7 us
  transfers between devices with their start and end apart: 3, of which 3 were waited for; matrix products, arithmetic and copies ran while one was open for 3% of the time, Pallas kernels for 0%

commit v1 on v0

--- a/solution.py
+++ b/solution.py
@@ -78,13 +78,10 @@
             payload.reshape(2, experts, 1, capacity, model_width),
             (2, experts, HALVES, capacity, model_width),
         )
-        arrived = lax.all_to_all(
-            spread.reshape(2, shards, capacity, model_width),
-            "expert",
-            split_axis=1,
-            concat_axis=1,
-            tiled=True,
-        )
+        block = spread.reshape(2, shards, capacity, model_width)
+        cells = jnp.split(block, lax.axis_size("expert"), axis=1)
+        arrived_2 = lax.all_to_all(jnp.stack(cells), "expert", 0, 0)
+        arrived = jnp.concatenate(arrived_2, axis=1)
         x_rows = arrived[0].reshape(shards * capacity, model_width)
         weighted = arrived[1].reshape(shards * capacity, model_width)
         partial_value, hidden, gate_rows, up_rows = rows_backward(

time: 672 us -> 688 us (1.024)
  local copies, waits for them, and re-layouts: 139 us -> 155 us
    unnamed x41 -> x103, local copies, waits for them, and re-layouts: 0.25 us -> 15.7 us
where the time goes in v1:
time: 688 us; the launch traced here: 682 us
  waiting for transfers between devices  239 us (35%)
  blocking collectives  177 us (26%)
  local copies, waits for them, and re-layouts  155 us (23%)
  matrix products  74 us (11%)
  starting transfers between devices  18.7 us (3%)
  other arithmetic  16.9 us (2%)
    all_to_all x2, waiting for transfers between devices, section_pass(): lax.all_to_all(partial_value, 'expert', split_axis=0, concat_axis=0, tile...  226 us
    all_to_all x2, blocking collectives, section_pass(): arrived_2 = lax.all_to_all(jnp.stack(cells), 'expert', 0, 0)  177 us
    slice x2, local copies, waits for them, and re-layouts, section_pass(): weighted = arrived[1].reshape(shards * capacity, model_width)  73.9 us
    all_to_all x2, starting transfers between devices, section_pass(): lax.all_to_all(partial_value, 'expert', split_axis=0, concat_axis=0, tile...  16.2 us
    unnamed x103, local copies, waits for them, and re-layouts  15.7 us
    broadcast_in_dim x2, local copies, waits for them, and re-layouts, section_pass(): jnp.broadcast_to(payload.reshape(2, experts, 1, capacity, model_width), (...  14.5 us
  transfers between devices with their start and end apart: 3, of which 3 were waited for; matrix products, arithmetic and copies ran while one was open for 3% of the time, Pallas kernels for 0%

profile of v1, /device:TPU:52, one launch (start us, length us, event | category | flops | bytes accessed | tf_op | source)
XLA Modules:
  0.0 682.5 jit_solution(15118912520696723312)
XLA Ops:
  13.5 7.4 %broadcast_in_dim.56 = bf16[2,16,2,14,4096]{4,0,3,2,1:T(2,128)(2,1)S(1)} broadcast(bf16[2,16,14,4096]{3,0,2,1:T(2,128)(2,1)S(1)} %bitcast.447), dimensions={0,1,3,4} | broadcast | bytes 11010048 | tf_op jit(solution)/shard_map/broadcast_in_dim | solution.py:77
  28.4 89.6 %all_to_all.20 = bf16[32,2,1,14,4096]{4,1,3,2,0:T(2,128)(2,1)S(1)} all-to-all(bf16[32,2,1,14,4096]{4,1,3,2,0:T(2,128)(2,1)S(1)} %fusion.64), channel_id=1, replica_groups=mesh['section'=4,'expert'=32] {'expert'}, dimensions={0} | all-to-all | bytes 14680064 | tf_op jit(solution)/shard_map/all_to_all | solution.py:83
  118.0 36.9 %slice_reduce_fusion.3 = (bf16[32,14,4096]{2,1,0:T(8,128)(2,1)}, bf16[32,14,4096]{2,1,0:T(8,128)(2,1)}) fusion(bf16[2,32,1,14,4096]{4,0,3,2,1:T(2,128)(2,1)S(1)} %bitcast.381), kind=kLoop, calls=%fused_computation.5 | loop fusion | bytes 14680064 | tf_op jit(solution)/shard_map/slice | solution.py:86
  154.9 5.0 reshape_squeeze.15
  159.9 5.1 fusion.10
  167.9 5.1 reshape_squeeze.14
  173.1 5.5 multiply_convert_fusion.4
  181.4 5.2 convolution_add_fusion.1
  186.6 6.9 %reshape.180 = f32[32,14,4096]{2,1,0:T(8,128)} reshape(f32[448,4096]{1,0:T(8,128)} %convolution_add_fusion.1) | data formatting | bytes 14680064 | tf_op jit(solution)/shard_map/reshape | solution.py:90
  193.5 8.0 %all-to-all-start.1 = ((f32[32,14,4096]{2,1,0:T(8,128)}), f32[32,14,4096]{2,1,0:T(8,128)}, u32[]{:S(2)}, u32[]{:S(2)}) async-start(f32[32,14,4096]{2,1,0:T(8,128)} %reshape.180), calls=%async_computation.1 | async-start | bytes 16777216 | tf_op jit(solution)/shard_map/all_to_all | solution.py:91
  201.6 124.2 %all-to-all-done.1 = f32[32,14,4096]{2,1,0:T(8,128)} async-done(((f32[32,14,4096]{2,1,0:T(8,128)}), f32[32,14,4096]{2,1,0:T(8,128)}, u32[]{:S(2)}, u32[]{:S(2)}) %all-to-all-start.1) | async-done | bytes 7340064 | tf_op jit(solution)/shard_map/all_to_all | solution.py:91
  325.8 6.0 bitcast_reduce_fusion.1
  340.2 12.8 %collective-permute-done = bf16[64,4096]{1,0:T(8,128)(2,1)} collective-permute-done((bf16[64,4096]{1,0:T(8,128)(2,1)}, bf16[64,4096]{1,0:T(8,128)(2,1)}, u32[]{:S(2)}, u32[]{:S(2)}) %collective-permute-start) | collective-permute-done | bytes 524320 | tf_op jit(solution)/shard_map/ppermute | solution.py:12
  360.2 7.1 %broadcast_in_dim.60 = bf16[2,16,2,14,4096]{4,0,3,2,1:T(2,128)(2,1)S(1)} broadcast(bf16[2,16,14,4096]{3,0,2,1:T(2,128)(2,1)S(1)} %bitcast.448), dimensions={0,1,3,4} | broadcast | bytes 11010048 | tf_op jit(solution)/shard_map/broadcast_in_dim | solution.py:77
  374.8 87.3 %all_to_all.21 = bf16[32,2,1,14,4096]{4,1,3,2,0:T(2,128)(2,1)S(1)} all-to-all(bf16[32,2,1,14,4096]{4,1,3,2,0:T(2,128)(2,1)S(1)} %fusion.32), channel_id=1, replica_groups=mesh['section'=4,'expert'=32] {'expert'}, dimensions={0} | all-to-all | bytes 14680064 | tf_op jit(solution)/shard_map/all_to_all | solution.py:83
  462.1 36.9 %slice_reduce_fusion.1 = (bf16[32,14,4096]{2,1,0:T(8,128)(2,1)}, bf16[32,14,4096]{2,1,0:T(8,128)(2,1)}) fusion(bf16[2,32,1,14,4096]{4,0,3,2,1:T(2,128)(2,1)S(1)} %bitcast.382), kind=kLoop, calls=%fused_computation.3 | loop fusion | bytes 14680064 | tf_op jit(solution)/shard_map/slice | solution.py:86
  499.0 5.0 reshape_squeeze.17
  504.0 6.1 fusion.13
  518.0 5.5 multiply_convert_fusion.2
  526.3 5.1 convolution_add_fusion
  531.4 6.8 %reshape.186 = f32[32,14,4096]{2,1,0:T(8,128)} reshape(f32[448,4096]{1,0:T(8,128)} %convolution_add_fusion) | data formatting | bytes 14680064 | tf_op jit(solution)/shard_map/reshape | solution.py:90
  538.3 8.2 %all-to-all-start.3 = ((f32[32,14,4096]{2,1,0:T(8,128)}), f32[32,14,4096]{2,1,0:T(8,128)}, u32[]{:S(2)}, u32[]{:S(2)}) async-start(f32[32,14,4096]{2,1,0:T(8,128)} %reshape.186), calls=%async_computation.3 | async-start | bytes 16777216 | tf_op jit(solution)/shard_map/all_to_all | solution.py:91
  568.3 102.3 %all-to-all-done.3 = f32[32,14,4096]{2,1,0:T(8,128)} async-done(((f32[32,14,4096]{2,1,0:T(8,128)}), f32[32,14,4096]{2,1,0:T(8,128)}, u32[]{:S(2)}, u32[]{:S(2)}) %all-to-all-start.3) | async-done | bytes 7340064 | tf_op jit(solution)/shard_map/all_to_all | solution.py:91
  670.6 6.1 bitcast_reduce_fusion
  (162 shorter events, 86.7 us)
Async XLA Ops:
  0.6 159.2 %copy-start = (bf16[1,1,4096,384]{3,2,1,0:T(8,128)(2,1)S(1)}, bf16[1,1,4096,384]{3,2,1,0:T(8,128)(2,1)}, u32[]{:S(2)}) copy-start(bf16[1,1,4096,384]{3,2,1,0:T(8,128)(2,1)} %param.13) | copy-start | bytes 9437188
  159.9 5.1 copy-start.3
  159.9 5.1 copy-start.7
  178.6 0.8 copy-start.12
  178.6 2.9 copy-start.8
  193.5 132.3 %all-to-all-start.1 = ((f32[32,14,4096]{2,1,0:T(8,128)}), f32[32,14,4096]{2,1,0:T(8,128)}, u32[]{:S(2)}, u32[]{:S(2)}) async-start(f32[32,14,4096]{2,1,0:T(8,128)} %reshape.180), calls=%async_computation.1 | async-start | bytes 16777216 | tf_op jit(solution)/shard_map/all_to_all | solution.py:91
  337.3 15.7 %collective-permute-start = (bf16[64,4096]{1,0:T(8,128)(2,1)}, bf16[64,4096]{1,0:T(8,128)(2,1)}, u32[]{:S(2)}, u32[]{:S(2)}) collective-permute-start(bf16[64,4096]{1,0:T(8,128)(2,1)} %fusion.3), channel_id=1, source_target_pairs={{32,0},{64,32},{96,64},{33,1},{65,33},{97,65},{34,2},{66,34},{98,6... | collective-permute-start | bytes 1572872 | tf_op jit(solution)/shard_map/ppermute | solution.py:12
  504.0 6.1 copy-start.1
  523.5 0.7 copy-start.14
  523.5 2.8 copy-start.10
  523.5 2.8 copy-start.9
  538.3 132.3 %all-to-all-start.3 = ((f32[32,14,4096]{2,1,0:T(8,128)}), f32[32,14,4096]{2,1,0:T(8,128)}, u32[]{:S(2)}, u32[]{:S(2)}) async-start(f32[32,14,4096]{2,1,0:T(8,128)} %reshape.186), calls=%async_computation.3 | async-start | bytes 16777216 | tf_op jit(solution)/shard_map/all_to_all | solution.py:91
  546.4 4.8 copy-start.4
  546.4 4.8 copy-start.13
  551.2 2.5 copy-start.5
  551.2 2.5 copy-start.16
  551.2 2.5 copy-start.17
  553.7 2.0 copy-start.2
  553.8 2.1 copy-start.11
  555.8 4.2 copy-start.15
  560.1 4.2 copy-start.6
  560.1 4.2 copy-start.18
  560.1 4.2 copy-start.19
